TPU v7x, 512 devices: a whole 4x8x8 slice. The times are simulated.
512 devices in a mesh: dp: 32 (over z_lo, y, core), tensor: 16 (over x, z_hi).
Axes of the slice: x: 4, y: 8, z: 8 (z_hi: 4, z_lo: 2; z = z_hi * 2 + z_lo), core: 2. Of those that a mesh axis runs over, the one named last changes fastest.
Arguments:
- queries: bfloat16 [16384, 8192], P('dp', 'tensor'), may hold values from -5 to 5
- keys: bfloat16 [16384, 1024], P('dp', 'tensor'), may hold values from -5 to 5
- values: bfloat16 [16384, 1024], P('dp', 'tensor'), may hold values from -6 to 6
- grad_out: bfloat16 [16384, 4096], P(('dp', 'tensor')), may hold values from -6 to 6
- out_weight: bfloat16 [4096, 8192], P('dp', 'tensor'), may hold values from -0.375 to 0.375
Outputs:
- grad_queries: bfloat16 [16384, 8192], P('dp', 'tensor')
- grad_keys: bfloat16 [16384, 1024], P('dp', 'tensor')
- grad_values: bfloat16 [16384, 1024], P('dp', 'tensor')
- grad_weight: bfloat16 [4096, 8192], P('dp', 'tensor')
All inputs are finite; a program needn't handle non-finite values.
Results may differ from a plain program's by a relative error of at most 0.03.
Values may be sent and summed in bfloat16 or wider, within the bound.
A program may use at most 64 MiB of HBM per device.

v0:
```python
import jax
import jax.numpy as jnp
from jax import lax
from jax.sharding import PartitionSpec as P

HEAD_DIM = 128


def partner(value, axis, apart):
    return lax.ppermute(value, axis, [(i, i ^ 1 << apart) for i in range(lax.axis_size(axis))])


def weight_gradient(grad_full, attended):
    return lax.psum_scatter(
        lax.dot_general(
            grad_full, attended, (((0,), (0,)), ((), ())), preferred_element_type=jnp.float32
        ).astype(jnp.bfloat16),
        "dp",
        scatter_dimension=0,
        tiled=True,
    )


def body(queries, keys, values, grad_out, out_weight):
    scale = HEAD_DIM ** (-0.5)
    half = HEAD_DIM // 2
    parity = lax.axis_index("tensor") % 2
    other_key, other_value = partner((keys, values), "tensor", 0)
    key_full = jnp.where(
        parity == 0, jnp.concatenate([keys, other_key], 1), jnp.concatenate([other_key, keys], 1)
    )
    value_full = jnp.where(
        parity == 0,
        jnp.concatenate([values, other_value], 1),
        jnp.concatenate([other_value, values], 1),
    )
    length = queries.shape[0]
    head_count = queries.shape[1] // HEAD_DIM
    query_heads = queries.reshape(length, head_count, HEAD_DIM)
    scores = (
        jnp.einsum("shd,td->hst", query_heads, key_full, preferred_element_type=jnp.float32) * scale
    )
    row_index = lax.broadcasted_iota(jnp.int32, (length, length), 0)
    column_index = lax.broadcasted_iota(jnp.int32, (length, length), 1)
    scores = jnp.where(column_index <= row_index, scores, -jnp.inf)
    probs = jax.nn.softmax(scores, axis=-1)
    probs_half = probs.astype(jnp.bfloat16)
    attended = jnp.einsum("hst,td->shd", probs_half, value_full, preferred_element_type=jnp.float32)
    attended = attended.astype(jnp.bfloat16).reshape(length, head_count * HEAD_DIM)
    grad_full = lax.all_gather(grad_out, "tensor", axis=0, tiled=True)
    grad_att = jnp.dot(
        grad_full,
        lax.all_gather(out_weight, "dp", axis=0, tiled=True),
        preferred_element_type=jnp.float32,
    ).astype(jnp.bfloat16)
    grad_heads = grad_att.reshape(length, head_count, HEAD_DIM)
    dprobs = jnp.einsum("shd,td->hst", grad_heads, value_full, preferred_element_type=jnp.float32)
    delta = jnp.sum(probs * dprobs, axis=-1, keepdims=True)
    dscores = (probs * (dprobs - delta) * scale).astype(jnp.bfloat16)
    grad_q = jnp.einsum("hst,td->shd", dscores, key_full, preferred_element_type=jnp.float32)
    grad_q = grad_q.astype(jnp.bfloat16).reshape(length, head_count * HEAD_DIM)
    key_part = jnp.einsum(
        "hst,shd->td", dscores, query_heads, preferred_element_type=jnp.float32
    ).astype(jnp.bfloat16)
    value_part = jnp.einsum(
        "hst,shd->td", probs_half, grad_heads, preferred_element_type=jnp.float32
    ).astype(jnp.bfloat16)
    partner_key, partner_value = partner((key_part, value_part), "tensor", 0)
    key_total = (key_part.astype(jnp.float32) + partner_key.astype(jnp.float32)).astype(
        jnp.bfloat16
    )
    value_total = (value_part.astype(jnp.float32) + partner_value.astype(jnp.float32)).astype(
        jnp.bfloat16
    )
    grad_k = lax.dynamic_slice_in_dim(key_total, parity * half, half, 1)
    grad_v = lax.dynamic_slice_in_dim(value_total, parity * half, half, 1)
    grad_weight = weight_gradient(grad_full, attended)
    return (grad_q, grad_k, grad_v, grad_weight)


def solution(mesh):
    placed = (
        P("dp", "tensor"),
        P("dp", "tensor"),
        P("dp", "tensor"),
        P(("dp", "tensor"), None),
        P("dp", "tensor"),
    )
    return jax.shard_map(
        body,
        mesh=mesh,
        in_specs=placed,
        out_specs=(P("dp", "tensor"), P("dp", "tensor"), P("dp", "tensor"), P("dp", "tensor")),
        check_vma=False,
    )
```

profile of v0, /device:TPU:2, one launch (start us, length us, event | category | flops | bytes accessed | tf_op | source)
XLA Modules:
  0.0 303.4 jit_solution(2214712308158737349)
XLA Ops:
  7.2 0.7 all-gather.3.cloned.1.call-update
  7.9 0.7 all-gather.5.cloned.1.call-update
  8.7 6.1 %collective-permute-start = (bf16[512,64]{0,1:T(8,128)(2,1)}, bf16[512,64]{0,1:T(8,128)(2,1)S(1)}, u32[]{:S(2)}, u32[]{:S(2)}) collective-permute-start(bf16[512,64]{0,1:T(8,128)(2,1)} %param.6), channel_id=1, source_target_pairs={{0,1},{1,0},{2,3},{3,2},{4,5},{5,4},{6,7},{7,6},{8,9},{9,8},{10,11... | collective-permute-start | bytes 196616 | tf_op jit(solution)/shard_map/ppermute | solution.py:10
  14.8 1.9 collective-permute-start.1
  16.7 1.3 copy.42
  18.0 0.1 iota_compare_fusion
  18.1 4.5 %fusion.47 = (f32[4,512]{1,0:T(4,128)S(1)}, f32[4,512,512]{1,2,0:T(8,128)}) fusion(pred[512,512]{0,1:T(8,128)(4,1)S(1)} %iota_compare_fusion, bf16[512,4,128]{0,2,1:T(8,128)(2,1)S(1)} %bitcast.92, bf16[512,64]{0,1:T(8,128)(2,1)S(1)} %collective-permute-done, bf16[512,64]{0,1:T(8,128)(2,1)} %param.6, pred[]{:T(512)S(6)} %eq.6), kind=kOutput, calls=%fused_computation.49 | convolution fusion | flops 273220096 | bytes 5120001 | tf_op jit(solution)/shard_map/sub | solution.py:46
  22.6 0.1 collective-permute-done.1
  22.8 2.7 convolution_convert_fusion.2
  25.4 74.2 %all-gather.3.cloned.1.call-done = bf16[512,4096]{1,0:T(8,128)(2,1)} async-done(((bf16[32,4096]{1,0:T(8,128)(2,1)}), bf16[512,4096]{1,0:T(8,128)(2,1)}) %all-gather.3.cloned.1.call-update) | async-done | bytes 4194320 | tf_op jit(solution)/shard_map/all_gather | solution.py:50
  99.7 6.5 %fusion.2 = bf16[4096,512]{0,1:T(8,128)(2,1)} fusion(bf16[512,512]{0,1:T(8,128)(2,1)S(1)} %bitcast.95, bf16[512,4096]{1,0:T(8,128)(2,1)} %all-gather.3.cloned.1.call-done), kind=kOutput, calls=%fused_computation.3 | convolution fusion | flops 2149580800 | bytes 8912896 | tf_op jit(solution)/shard_map/dot_general | solution.py:15
  106.1 6.5 %copy.40 = bf16[4096,512]{1,0:T(8,128)(2,1)} copy(bf16[4096,512]{0,1:T(8,128)(2,1)} %fusion.2) | data formatting | bytes 8388608
  112.7 56.5 %all-gather.5.cloned.1.call-done = bf16[4096,512]{1,0:T(8,128)(2,1)} async-done(((bf16[128,512]{1,0:T(8,128)(2,1)}), bf16[4096,512]{1,0:T(8,128)(2,1)}) %all-gather.5.cloned.1.call-update) | async-done | bytes 4194320 | tf_op jit(solution)/shard_map/all_gather | solution.py:53
  169.2 6.0 %convolution_convert_fusion.1 = bf16[512,512]{0,1:T(8,128)(2,1)S(1)} fusion(bf16[512,4096]{1,0:T(8,128)(2,1)} %all-gather.3.cloned.1.call-done, bf16[4096,512]{1,0:T(8,128)(2,1)} %all-gather.5.cloned.1.call-done), kind=kOutput, calls=%fused_computation.20 | convolution fusion | flops 2147745792 | bytes 8912896 | tf_op jit(solution)/shard_map/dot_general | solution.py:51
  175.2 0.8 fusion.16
  176.0 4.6 %collective-permute-start.3 = (bf16[512,128]{0,1:T(8,128)(2,1)S(1)}, bf16[512,128]{0,1:T(8,128)(2,1)S(1)}, u32[]{:S(2)}, u32[]{:S(2)}) collective-permute-start(bf16[512,128]{0,1:T(8,128)(2,1)S(1)} %fusion.16), channel_id=1, source_target_pairs={{0,1},{1,0},{2,3},{3,2},{4,5},{5,4},{6,7},{7,6},{8,9},{9,8},{10,11... | collective-permute-start | bytes 393224 | tf_op jit(solution)/shard_map/ppermute | solution.py:10
  180.7 2.7 fusion.24
  183.4 7.6 %fusion.15 = bf16[512,128]{0,1:T(8,128)(2,1)S(1)} fusion(bf16[512,4,128]{0,2,1:T(8,128)(2,1)S(1)} %bitcast.93, f32[512,512,4]{1,0,2:T(8,128)} %fusion.24, f32[4,512,512]{1,2,0:T(8,128)} %get-tuple-element.13, f32[4,512]{1,0:T(4,128)S(1)} %get-tuple-element.12), kind=kOutput, calls=%fused_computation.24 | convolution fusion | flops 275843584 | bytes 9052160 | tf_op jit(solution)/shard_map/hst,shd->td/dot_general | solution.py:62
  191.0 2.1 collective-permute-start.2
  193.1 7.8 %fusion.13 = bf16[128,4,512]{2,0,1:T(8,128)(2,1)S(1)} fusion(f32[512,512,4]{1,0,2:T(8,128)} %fusion.24, bf16[512,64]{0,1:T(8,128)(2,1)S(1)} %collective-permute-done, bf16[512,64]{0,1:T(8,128)(2,1)S(1)} %copy-done.1, pred[]{:T(512)S(6)} %eq.6, f32[4,512,512]{1,2,0:T(8,128)} %get-tuple-element.13, f32[4,512]{1,0:T(4,128)S(1)} %get-tuple-element.12), kind=kOutput, calls=%fused_computation.19 | convolution fusion | flops 276630016 | bytes 9052161 | tf_op jit(solution)/shard_map/hst,td->shd/dot_general | solution.py:60
  200.9 1.0 copy.29
  201.9 0.6 add_convert_fusion
  202.5 0.6 add_convert_fusion.1
  203.2 93.6 %reduce-scatter.4.cloned.1.call-done = bf16[128,512]{1,0:T(8,128)(2,1)} async-done(((bf16[4096,512]{1,0:T(8,128)(2,1)}), bf16[128,512]{1,0:T(8,128)(2,1)}) %reduce-scatter.4.cloned.1.call-update) | async-done | bytes 131088
  (13 shorter events, 0.2 us)
Async XLA Ops:
  7.2 92.5 %all-gather.3.cloned.1.call-start = ((), (), s32[]{:S(2)}) async-start(), calls=%async_computation.1 | async-start | bytes 4456448 | tf_op jit(solution)/shard_map/all_gather | solution.py:50
  7.9 161.3 %all-gather.5.cloned.1.call-start = ((), (), s32[]{:S(2)}) async-start(), calls=%async_computation.2 | async-start | bytes 4325376 | tf_op jit(solution)/shard_map/all_gather | solution.py:53
  8.6 288.2 %reduce-scatter.4.cloned.1.call-start = ((), (), s32[]{:S(2)}) async-start(), calls=%async_computation.3 | async-start | bytes 4325376
  8.7 9.4 %collective-permute-start = (bf16[512,64]{0,1:T(8,128)(2,1)}, bf16[512,64]{0,1:T(8,128)(2,1)S(1)}, u32[]{:S(2)}, u32[]{:S(2)}) collective-permute-start(bf16[512,64]{0,1:T(8,128)(2,1)} %param.6), channel_id=1, source_target_pairs={{0,1},{1,0},{2,3},{3,2},{4,5},{5,4},{6,7},{7,6},{8,9},{9,8},{10,11... | collective-permute-start | bytes 196616 | tf_op jit(solution)/shard_map/ppermute | solution.py:10
  14.8 8.0 %collective-permute-start.1 = (bf16[512,64]{0,1:T(8,128)(2,1)}, bf16[512,64]{0,1:T(8,128)(2,1)S(1)}, u32[]{:S(2)}, u32[]{:S(2)}) collective-permute-start(bf16[512,64]{0,1:T(8,128)(2,1)} %param.7), channel_id=1, source_target_pairs={{0,1},{1,0},{2,3},{3,2},{4,5},{5,4},{6,7},{7,6},{8,9},{9,8},{10,11... | collective-permute-start | bytes 196616 | tf_op jit(solution)/shard_map/ppermute | solution.py:10
  18.1 4.7 %copy-start = (bf16[512,64]{0,1:T(8,128)(2,1)S(1)}, bf16[512,64]{0,1:T(8,128)(2,1)}, u32[]{:S(2)}) copy-start(bf16[512,64]{0,1:T(8,128)(2,1)} %param.7) | copy-start | bytes 196612
  169.2 6.0 %copy-start.2 = (f32[4,512,512]{1,2,0:T(8,128)S(1)}, f32[4,512,512]{1,2,0:T(8,128)}, u32[]{:S(2)}) copy-start(f32[4,512,512]{1,2,0:T(8,128)} %get-tuple-element.13) | copy-start | bytes 12582916
  176.0 25.9 %collective-permute-start.3 = (bf16[512,128]{0,1:T(8,128)(2,1)S(1)}, bf16[512,128]{0,1:T(8,128)(2,1)S(1)}, u32[]{:S(2)}, u32[]{:S(2)}) collective-permute-start(bf16[512,128]{0,1:T(8,128)(2,1)S(1)} %fusion.16), channel_id=1, source_target_pairs={{0,1},{1,0},{2,3},{3,2},{4,5},{5,4},{6,7},{7,6},{8,9},{9,8},{10,11... | collective-permute-start | bytes 393224 | tf_op jit(solution)/shard_map/ppermute | solution.py:10
  183.4 9.7 %copy-start.1 = (bf16[512,64]{0,1:T(8,128)(2,1)S(1)}, bf16[512,64]{0,1:T(8,128)(2,1)}, u32[]{:S(2)}) copy-start(bf16[512,64]{0,1:T(8,128)(2,1)} %param.6) | copy-start | bytes 196612
  191.0 11.5 %collective-permute-start.2 = (bf16[512,128]{0,1:T(8,128)(2,1)S(1)}, bf16[512,128]{0,1:T(8,128)(2,1)S(1)}, u32[]{:S(2)}, u32[]{:S(2)}) collective-permute-start(bf16[512,128]{0,1:T(8,128)(2,1)S(1)} %fusion.15), channel_id=1, source_target_pairs={{0,1},{1,0},{2,3},{3,2},{4,5},{5,4},{6,7},{7,6},{8,9},{9,8},{10,11... | collective-permute-start | bytes 393224 | tf_op jit(solution)/shard_map/ppermute | solution.py:10
Sparse Core Ops, SparseCore 0:
  11.0 88.6 all-gather.2
  101.8 67.3 all-gather.4
  172.6 124.1 reduce-scatter.3
where the time goes:
time: 304 us; the launch traced here: 303 us
  waiting for transfers between devices  226 us (74%)
  matrix products  38.5 us (13%)
  starting transfers between devices  14.9 us (5%)
  between operations  13.9 us (5%)
  local copies, waits for them, and re-layouts  8.8 us (3%)
    unnamed x4, waiting for transfers between devices  95 us
    all_gather x1, waiting for transfers between devices, body(): grad_full = lax.all_gather(grad_out, 'tensor', axis=0, tiled=True)  74.2 us
    all_gather x1, waiting for transfers between devices, body(): lax.all_gather(out_weight, 'dp', axis=0, tiled=True)  56.5 us
    ppermute x4, starting transfers between devices, partner(): lax.ppermute(value, axis, [(i, i ^ 1 << apart) for i in range(lax.axis_si...  14.7 us
    dot_general x1, matrix products, body(): jnp.einsum('hst,td->shd', dscores, key_full, preferred_element_type=jnp.f...  7.77 us
    dot_general x1, matrix products, body(): jnp.einsum('hst,shd->td', dscores, query_heads, preferred_element_type=jn...  7.61 us
    unnamed x8, local copies, waits for them, and re-layouts  7.54 us
    dot_general x1, matrix products, weight_gradient(): lax.dot_general(grad_full, attended, (((0,), (0,)), ((), ())), preferred_...  6.47 us
  transfers between devices with their start and end apart: 7, of which 4 were waited for; matrix products, arithmetic and copies ran while one was open for 16% of the time, Pallas kernels for 0%

commit v1 on v0

v1 whole, which is shorter than its diff:
```python
import jax
import jax.numpy as jnp
from jax import lax
from jax.experimental import pallas as pl
from jax.experimental.pallas import tpu as pltpu
from jax.sharding import PartitionSpec as P

HEAD_DIM = 128
MESH = pl.DeviceIdType.MESH
F32 = jnp.float32
BF16 = jnp.bfloat16

ORDER = (4, 3, -3, 2, -2, 1, -1, 0)
AT = {relative: place for place, relative in enumerate(ORDER)}
AT[-4] = AT[4]
ABOVE = 8

NX, NZ, NY = 4, 4, 8
N_COPIES = 160


def nt(a, b):
    return lax.dot_general(a, b, (((1,), (1,)), ((), ())), preferred_element_type=F32)


def nn(a, b):
    return lax.dot_general(a, b, (((1,), (0,)), ((), ())), preferred_element_type=F32)


def kernel(
    q_ref, k_ref, v_ref, g_ref, w_ref,
    gq_ref, gk_ref, gv_ref, gw_ref,
    gbuf, wbuf, kv_send, kv_recv, k_full, v_full, k_turned, v_turned,
    probs, att, total, grad_att, terms, core_send, core_recv, y_send, y_recv,
    z_send, z_recv, key_acc, value_acc, part_send, part_recv, send_sem, recv_sem,
):
    scale = HEAD_DIM ** (-0.5)
    dp = lax.axis_index("dp")
    tensor = lax.axis_index("tensor")
    core = lax.rem(dp, 2)
    y = lax.rem(dp // 2, NY)
    zl = dp // (2 * NY)
    x = tensor // NZ
    zh = lax.rem(tensor, NZ)
    parity = lax.rem(tensor, 2)

    def device(core=core, y=y, zl=zl, x=x, zh=zh):
        return ((zl * NY + y) * 2 + core, x * NZ + zh)

    x_up, x_down = lax.rem(x + 1, NX), lax.rem(x + NX - 1, NX)
    z_up, z_down = lax.rem(zh + 1, NZ), lax.rem(zh + NZ - 1, NZ)
    to_x_up, to_x_down = device(x=x_up), device(x=x_down)
    to_z_up, to_z_down = device(zh=z_up), device(zh=z_down)
    to_y_up = device(y=lax.rem(y + 1, NY))
    to_y_down = device(y=lax.rem(y + NY - 1, NY))
    to_pair = device(zl=1 - zl)
    to_core = device(core=1 - core)
    to_partner = (dp, tensor + 1 - 2 * parity)

    barrier = pltpu.get_barrier_semaphore()
    for target in (to_x_up, to_x_down, to_z_up, to_z_down, to_y_up, to_y_down, to_pair, to_core):
        pl.semaphore_signal(barrier, inc=1, device_id=target, device_id_type=MESH)

    copies, started = {}, []

    def send(name, source, target, to):
        index = len(started)
        started.append(name)
        copy = pltpu.make_async_remote_copy(
            src_ref=source, dst_ref=target, send_sem=send_sem.at[index], recv_sem=recv_sem.at[index],
            device_id=to, device_id_type=MESH,
        )
        copy.start()
        copies[name] = copy

    def arrived(name):
        copies[name].wait_recv()

    kv_send[...] = jnp.concatenate([k_ref[...], v_ref[...]], 1)
    wbuf[AT[0], 2 + zl] = w_ref[...]
    own_rows = pl.ds(pl.multiple_of(zh * 32, 32), 32)
    for place, relative in enumerate(ORDER):
        column = lax.rem(y + relative + NY, NY)
        for slot in range(4):
            of_core = core if slot >= 2 else 1 - core
            block = ((slot % 2) * NY + column) * 2 + of_core
            gbuf[place, x, own_rows, slot * 128 : (slot + 1) * 128] = g_ref[
                :, pl.ds(pl.multiple_of(block * 128, 128), 128)
            ]
    pl.semaphore_wait(barrier, 8)

    def z_rows(at, first, count):
        return pl.ds(pl.multiple_of(at * 32 + first, 16), count)

    def g_z1(place):
        block = gbuf.at[place, x, z_rows(zh, 0, 32)]
        send(("z1u", place), block, block, to_z_up)
        send(("z1d", place), block, block, to_z_down)

    def g_z2(place):
        arrived(("z1u", place))
        block = gbuf.at[place, x, z_rows(z_down, 0, 16)]
        send(("z2u", place), block, block, to_z_up)
        arrived(("z1d", place))
        block = gbuf.at[place, x, z_rows(z_up, 16, 16)]
        send(("z2d", place), block, block, to_z_down)

    def g_x1(place):
        arrived(("z2u", place))
        arrived(("z2d", place))
        block = gbuf.at[place, x]
        send(("x1u", place), block, block, to_x_up)
        send(("x1d", place), block, block, to_x_down)

    def g_x2(place):
        arrived(("x1u", place))
        block = gbuf.at[place, x_down, 0:64]
        send(("x2u", place), block, block, to_x_up)
        arrived(("x1d", place))
        block = gbuf.at[place, x_up, 64:128]
        send(("x2d", place), block, block, to_x_down)

    def g_done(place):
        arrived(("x2u", place))
        arrived(("x2d", place))

    row = {"a": 2 + zl, "b": 3 - zl}

    def w_hop(block, step, up):
        relative = (1 - step) if up else (step - 1)
        source = wbuf.at[AT[relative], row[block]]
        target = wbuf.at[AT[relative - 1 if up else relative + 1], row[block]]
        send(("w", block, step, up), source, target, to_y_up if up else to_y_down)

    def w_start():
        w_hop("a", 1, True)
        w_hop("a", 1, False)
        own = wbuf.at[AT[0], row["a"]]
        send("wz", own, own, to_pair)

    def w_core(relative):
        send(
            ("wc", AT[relative]), wbuf.at[AT[relative], 2:4], wbuf.at[AT[relative], 0:2], to_core
        )

    def w_pair():
        arrived("wz")
        w_hop("b", 1, True)
        w_hop("b", 1, False)
        w_core(0)

    def w_next(block, step):
        for up in (True, False):
            arrived(("w", block, step, up))
            if step < 3 or (block == "a") == up:
                w_hop(block, step + 1, up)
        if block == "b":
            w_core(step)
            w_core(-step)

    def w_last():
        arrived(("w", "a", 4, True))
        arrived(("w", "b", 4, False))
        w_core(4)

    def spans():
        for part in range(2):
            yield slice(part * 256, part * 256 + 256), (part + 1) * 256

    def kv_ready():
        arrived("kv")
        first = jnp.where(parity == 0, kv_send[...], kv_recv[...])
        second = jnp.where(parity == 0, kv_recv[...], kv_send[...])
        key = jnp.concatenate([first[:, 0:64], second[:, 0:64]], 1)
        value = jnp.concatenate([first[:, 64:128], second[:, 64:128]], 1)
        k_full[...] = key
        v_full[...] = value
        k_turned[...] = key.astype(F32).T.astype(BF16)
        v_turned[...] = value.astype(F32).T.astype(BF16)

    def forward(head):
        columns = slice(head * 128, head * 128 + 128)
        for span, length in spans():
            scores = nt(k_full[0:length], q_ref[span, columns]) * scale
            key_at = lax.broadcasted_iota(jnp.int32, (length, 256), 0)
            query_at = lax.broadcasted_iota(jnp.int32, (length, 256), 1) + (length - 256)
            scores = jnp.where(key_at <= query_at, scores, -jnp.inf)
            powers = jnp.exp(scores - jnp.max(scores, axis=0, keepdims=True))
            part = powers * (1.0 / jnp.sum(powers, axis=0, keepdims=True))
            probs[head, 0:length, span] = part
            att[columns, span] = nn(v_turned[:, 0:length], part.astype(BF16)).astype(BF16)

    def backward(head):
        columns = slice(head * 128, head * 128 + 128)
        for span, length in spans():
            grad = grad_att[span, columns]
            part = probs[head, 0:length, span]
            dprobs = nt(v_full[0:length], grad)
            delta = jnp.sum(part * dprobs, axis=0, keepdims=True)
            dscores = (part * (dprobs - delta) * scale).astype(BF16)
            gq_ref[span, columns] = nn(k_turned[:, 0:length], dscores).T.astype(BF16)
            key_part = nn(dscores, q_ref[span, columns])
            value_part = nn(part.astype(BF16), grad)
            if head == 0 and length == 256:
                key_acc[256:512] = jnp.zeros((256, 128), F32)
                value_acc[256:512] = jnp.zeros((256, 128), F32)
                key_acc[0:256] = key_part
                value_acc[0:256] = value_part
            else:
                key_acc[0:length] += key_part
                value_acc[0:length] += value_part

    def parts_send():
        key, value = key_acc[...].astype(BF16), value_acc[...].astype(BF16)
        low = jnp.concatenate([key[:, 0:64], value[:, 0:64]], 1)
        high = jnp.concatenate([key[:, 64:128], value[:, 64:128]], 1)
        part_send[...] = jnp.where(parity == 0, high, low)
        copies.pop("kv").wait_send()
        kv_send[...] = jnp.where(parity == 0, low, high)
        send("parts", part_send, part_recv, to_partner)

    def parts_done():
        arrived("parts")
        both = (kv_send[...].astype(F32) + part_recv[...].astype(F32)).astype(BF16)
        gk_ref[...] = both[:, 0:64]
        gv_ref[...] = both[:, 64:128]

    def gather_term(place):
        arrived(("wc", place))
        for half in range(2):
            columns = slice(half * 256, half * 256 + 256)
            product = nn(
                gbuf[place].reshape(512, 512), wbuf[place, :, :, columns].reshape(512, 256)
            )
            if place == 0:
                total[:, columns] = product
            else:
                total[:, columns] += product
            if place == 7:
                grad_att[:, columns] = total[:, columns].astype(BF16)

    def weight_term(place):
        features = gbuf[place].reshape(512, 512)
        product = nn(att[...], features[:, 0:256])
        core_send[place, 0] = product[:, 0:128].astype(BF16)
        core_send[place, 1] = product[:, 128:256].astype(BF16)
        send(("core", place), core_send.at[place], core_recv.at[place], to_core)
        terms[place] = nn(att[...], features[:, 256:512])

    def ring(place):
        relative = ORDER[place]
        arrived(("core", place))
        if relative != 4:
            if relative >= 0:
                arrived(("ring", relative + 1, True))
            if relative <= 0:
                arrived(("ring", relative - 1, False))
        for at in range(2):
            partial = terms[place, :, at * 128 : at * 128 + 128] + core_recv[place, at].astype(F32)
            if relative == 3 and at == 0 or relative == -3 and at == 1 or 0 < abs(relative) < 3:
                partial += y_recv[place, at].astype(F32)
            if relative == 0:
                partial += y_recv[place, at].astype(F32) + y_recv[ABOVE, at].astype(F32)
                terms[place, :, at * 128 : at * 128 + 128] = partial
            else:
                y_send[place, at] = partial.astype(BF16)
        if relative == 4:
            send(("ring", 4, True), y_send.at[place, 0], y_recv.at[AT[3], 0], to_y_up)
            send(("ring", -4, False), y_send.at[place, 1], y_recv.at[AT[-3], 1], to_y_down)
        elif relative > 0:
            send(("ring", relative, True), y_send.at[place], y_recv.at[AT[relative - 1]], to_y_up)
        elif relative < 0:
            slot = ABOVE if relative == -1 else AT[relative + 1]
            send(("ring", relative, False), y_send.at[place], y_recv.at[slot], to_y_down)
        else:
            low, high = terms[place, :, 0:128], terms[place, :, 128:256]
            z_send[...] = jnp.where(zl == 0, high, low).astype(BF16)
            send("pair", z_send, z_recv, to_pair)

    def ring_done():
        arrived("pair")
        low, high = terms[AT[0], :, 0:128], terms[AT[0], :, 128:256]
        final = jnp.where(zl == 0, low, high) + z_recv[...].astype(F32)
        gw_ref[...] = final.T.astype(BF16)

    send("kv", kv_send, kv_recv, to_partner)
    w_start()
    g_z1(0)
    g_z1(1)
    g_z1(2)
    g_z2(0)
    g_x1(0)
    w_pair()
    g_z2(1)
    g_z1(3)
    kv_ready()
    g_x1(1)
    forward(0)
    w_next("a", 1)
    g_x2(0)
    forward(1)
    g_z2(2)
    g_z1(4)
    g_x1(2)
    w_next("b", 1)
    forward(2)
    g_x2(1)
    w_next("a", 2)
    forward(3)
    g_z2(3)
    g_z1(5)
    g_done(0)
    weight_term(0)
    g_x1(3)
    w_next("b", 2)
    ring(0)
    g_x2(2)
    w_next("a", 3)
    g_z2(4)
    g_z1(6)
    g_done(1)
    weight_term(1)
    g_x1(4)
    w_next("b", 3)
    g_x2(3)
    ring(1)
    g_done(2)
    weight_term(2)
    g_z2(5)
    g_z1(7)
    g_x1(5)
    w_last()
    ring(2)
    g_x2(4)
    gather_term(0)
    gather_term(1)
    gather_term(2)
    g_done(3)
    weight_term(3)
    g_z2(6)
    g_x1(6)
    g_x2(5)
    gather_term(3)
    ring(3)
    g_done(4)
    weight_term(4)
    g_z2(7)
    g_x1(7)
    g_x2(6)
    gather_term(4)
    ring(4)
    g_done(5)
    weight_term(5)
    gather_term(5)
    g_x2(7)
    ring(5)
    g_done(6)
    weight_term(6)
    gather_term(6)
    ring(6)
    g_done(7)
    weight_term(7)
    gather_term(7)
    backward(0)
    ring(7)
    backward(1)
    backward(2)
    backward(3)
    parts_send()
    ring_done()
    parts_done()
    for copy in copies.values():
        copy.wait_send()


def body(queries, keys, values, grad_out, out_weight):
    vmem = pl.BlockSpec(memory_space=pltpu.VMEM)
    return pl.pallas_call(
        kernel,
        out_shape=(
            jax.ShapeDtypeStruct((512, 512), BF16),
            jax.ShapeDtypeStruct((512, 64), BF16),
            jax.ShapeDtypeStruct((512, 64), BF16),
            jax.ShapeDtypeStruct((128, 512), BF16),
        ),
        in_specs=[vmem] * 5,
        out_specs=(vmem,) * 4,
        scratch_shapes=[
            pltpu.VMEM((8, 4, 128, 512), BF16),
            pltpu.VMEM((8, 4, 128, 512), BF16),
            pltpu.VMEM((512, 128), BF16),
            pltpu.VMEM((512, 128), BF16),
            pltpu.VMEM((512, 128), BF16),
            pltpu.VMEM((512, 128), BF16),
            pltpu.VMEM((128, 512), BF16),
            pltpu.VMEM((128, 512), BF16),
            pltpu.VMEM((4, 512, 512), F32),
            pltpu.VMEM((512, 512), BF16),
            pltpu.VMEM((512, 512), F32),
            pltpu.VMEM((512, 512), BF16),
            pltpu.VMEM((8, 512, 256), F32),
            pltpu.VMEM((8, 2, 512, 128), BF16),
            pltpu.VMEM((8, 2, 512, 128), BF16),
            pltpu.VMEM((8, 2, 512, 128), BF16),
            pltpu.VMEM((9, 2, 512, 128), BF16),
            pltpu.VMEM((512, 128), BF16),
            pltpu.VMEM((512, 128), BF16),
            pltpu.VMEM((512, 128), F32),
            pltpu.VMEM((512, 128), F32),
            pltpu.VMEM((512, 128), BF16),
            pltpu.VMEM((512, 128), BF16),
            pltpu.SemaphoreType.DMA((N_COPIES,)),
            pltpu.SemaphoreType.DMA((N_COPIES,)),
        ],
        compiler_params=pltpu.CompilerParams(
            collective_id=0, has_side_effects=True, vmem_limit_bytes=56 * 1024 * 1024
        ),
        cost_estimate=pl.CostEstimate(
            flops=6_000_000_000, bytes_accessed=4_000_000, transcendentals=1_000_000
        ),
    )(queries, keys, values, grad_out, out_weight)


def solution(mesh):
    placed = (
        P("dp", "tensor"),
        P("dp", "tensor"),
        P("dp", "tensor"),
        P(("dp", "tensor"), None),
        P("dp", "tensor"),
    )
    return jax.shard_map(
        body,
        mesh=mesh,
        in_specs=placed,
        out_specs=(P("dp", "tensor"), P("dp", "tensor"), P("dp", "tensor"), P("dp", "tensor")),
        check_vma=False,
    )
```

time: 304 us -> 106 us (0.35)
  the two profiles are of different devices: /device:TPU:2 before, /device:TPU:25 now
where the time goes in v1:
time: 106 us; the launch traced here: 105 us
  Pallas kernels  97.5 us (92%)
  local copies, waits for them, and re-layouts  7.35 us (7%)
    pallas_call x1, Pallas kernels, body(): pl.pallas_call(kernel, out_shape=(jax.ShapeDtypeStruct((512, 512), BF16),...  97.5 us
    unnamed x10, local copies, waits for them, and re-layouts  4.96 us
    pallas_call x2, local copies, waits for them, and re-layouts, body(): pl.pallas_call(kernel, out_shape=(jax.ShapeDtypeStruct((512, 512), BF16),...  2.38 us

profile of v1, /device:TPU:25, one launch (start us, length us, event | category | flops | bytes accessed | tf_op | source)
XLA Modules:
  0.0 105.5 jit_solution(17783692960257238243)
XLA Ops:
  0.6 0.0 copy-start.2
  0.6 1.6 %copy.9.k_ref = bf16[512,64]{1,0:T(8,128)(2,1)} copy(bf16[512,64]{0,1:T(8,128)(2,1)} %param.6) | data formatting | bytes 131072 | tf_op args[1]
  2.3 0.0 copy-done.2
  2.3 0.8 copy.10.v_ref
  3.0 97.5 %shard_map.84 = (bf16[512,512]{1,0:T(8,128)(2,1)}, bf16[512,64]{1,0:T(8,128)(2,1)}, bf16[512,64]{1,0:T(8,128)(2,1)}, bf16[128,512]{1,0:T(8,128)(2,1)}) custom-call(bf16[512,512]{1,0:T(8,128)(2,1)} %q_ref.1, bf16[512,64]{1,0:T(8,128)(2,1)} %copy.9.k_ref, bf16[512,64]{1,0:T(8,128)(2,1)} %copy.10.v_ref, bf16[32,4096]{1,0:T(8,128)(2,1)} %g_ref.1, ...), custom_call_target="tpu_custom_call" | custom-call | flops 6000000000 | bytes 4000000 | tf_op jit(solution)/shard_map/pallas_call | solution.py:378
  100.5 0.0 copy-start
  100.5 1.7 %copy.11 = bf16[512,64]{0,1:T(8,128)(2,1)} copy(bf16[512,64]{1,0:T(8,128)(2,1)} %get-tuple-element.5) | data formatting | bytes 131072 | tf_op jit(solution)/shard_map/pallas_call | solution.py:378
  102.2 0.0 copy-done
  102.2 0.7 copy.12
  102.9 0.0 copy-start.1
  102.9 1.9 %copy.15 = bf16[512,512]{1,0:T(8,128)(2,1)} copy(bf16[512,512]{1,0:T(8,128)(2,1)} %get-tuple-element.12) | data formatting | bytes 1048576
  104.8 0.0 copy-done.1
  104.8 0.7 copy.16
Async XLA Ops:
  0.6 1.6 %copy-start.2 = (bf16[512,64]{0,1:T(8,128)(2,1)S(1)}, bf16[512,64]{0,1:T(8,128)(2,1)}, u32[]{:S(2)}) copy-start(bf16[512,64]{0,1:T(8,128)(2,1)} %param.7) | copy-start | bytes 196612
  100.5 1.7 %copy-start = (bf16[512,64]{1,0:T(8,128)(2,1)S(1)}, bf16[512,64]{1,0:T(8,128)(2,1)}, u32[]{:S(2)}) copy-start(bf16[512,64]{1,0:T(8,128)(2,1)} %get-tuple-element.6) | copy-start | bytes 196612
  102.9 1.9 %copy-start.1 = (bf16[128,512]{1,0:T(8,128)(2,1)S(1)}, bf16[128,512]{1,0:T(8,128)(2,1)}, u32[]{:S(2)}) copy-start(bf16[128,512]{1,0:T(8,128)(2,1)} %get-tuple-element.15) | copy-start | bytes 393220

commit v2 on v1

v2 whole, which is shorter than its diff:
```python
import jax
import jax.numpy as jnp
from jax import lax
from jax.experimental import pallas as pl
from jax.experimental.pallas import tpu as pltpu
from jax.sharding import PartitionSpec as P

HEAD_DIM = 128
MESH = pl.DeviceIdType.MESH
F32 = jnp.float32
BF16 = jnp.bfloat16

ORDER = (4, 3, -3, 2, -2, 1, -1, 0)
AT = {relative: place for place, relative in enumerate(ORDER)}
AT[-4] = AT[4]
ABOVE = 8

NX, NZ, NY = 4, 4, 8
N_COPIES = 208

WAY = tuple('PPPPPPZZ')


def nt(a, b):
    return lax.dot_general(a, b, (((1,), (1,)), ((), ())), preferred_element_type=F32)


def nn(a, b):
    return lax.dot_general(a, b, (((1,), (0,)), ((), ())), preferred_element_type=F32)


def kernel(
    q_ref, k_ref, v_ref, g_ref, w_ref,
    gq_ref, gk_ref, gv_ref, gw_ref,
    gbuf, wbuf, kv_send, kv_recv, k_full, v_full, k_turned, v_turned,
    probs, att, total, grad_att, terms, core_send, core_recv, y_send, y_recv,
    z_send, z_recv, key_acc, value_acc, key_part, value_part, key_recv, value_recv, send_sem, recv_sem,
):
    scale = HEAD_DIM ** (-0.5)
    dp = lax.axis_index("dp")
    tensor = lax.axis_index("tensor")
    core = lax.rem(dp, 2)
    y = lax.rem(dp // 2, NY)
    zl = dp // (2 * NY)
    x = tensor // NZ
    zh = lax.rem(tensor, NZ)
    parity = lax.rem(tensor, 2)

    def device(core=core, y=y, zl=zl, x=x, zh=zh):
        return ((zl * NY + y) * 2 + core, x * NZ + zh)

    x_up, x_down = lax.rem(x + 1, NX), lax.rem(x + NX - 1, NX)
    z_up, z_down = lax.rem(zh + 1, NZ), lax.rem(zh + NZ - 1, NZ)
    to_x_up, to_x_down = device(x=x_up), device(x=x_down)
    to_z_up, to_z_down = device(zh=z_up), device(zh=z_down)
    to_y_up = device(y=lax.rem(y + 1, NY))
    to_y_down = device(y=lax.rem(y + NY - 1, NY))
    to_pair = device(zl=1 - zl)
    to_core = device(core=1 - core)
    to_partner = (dp, tensor + 1 - 2 * parity)

    barrier = pltpu.get_barrier_semaphore()
    for target in (to_x_up, to_x_down, to_z_up, to_z_down, to_y_up, to_y_down, to_pair, to_core):
        pl.semaphore_signal(barrier, inc=1, device_id=target, device_id_type=MESH)

    copies = {}

    def send(name, source, target, to):
        index = len(copies)
        copy = pltpu.make_async_remote_copy(
            src_ref=source, dst_ref=target, send_sem=send_sem.at[index], recv_sem=recv_sem.at[index],
            device_id=to, device_id_type=MESH,
        )
        copy.start()
        copies[name] = copy

    waited = set()

    def arrived(*names):
        for name in names:
            if name not in waited:
                copies[name].wait_recv()
                waited.add(name)

    kv_send[0:64] = k_ref[...]
    kv_send[64:128] = v_ref[...]
    wbuf[AT[0], 2 + zl] = w_ref[...]
    own_rows = pl.ds(pl.multiple_of(zh * 32, 32), 32)
    for place, relative in enumerate(ORDER):
        column = lax.rem(y + relative + NY, NY)
        for slot in range(4):
            of_core = core if slot >= 2 else 1 - core
            block = ((slot % 2) * NY + column) * 2 + of_core
            gbuf[place, x, own_rows, slot * 128 : (slot + 1) * 128] = g_ref[
                :, pl.ds(pl.multiple_of(block * 128, 128), 128)
            ]
    pl.semaphore_wait(barrier, 8)

    def z_rows(at, first, count):
        return pl.ds(pl.multiple_of(at * 32 + first, 16), count)

    to_x, to_y, to_z = (
        {"u": to_x_up, "d": to_x_down}, {"u": to_y_up, "d": to_y_down}, {"u": to_z_up, "d": to_z_down},
    )
    from_x, from_z = {"u": x_down, "d": x_up}, {"u": z_down, "d": z_up}
    kept = {"u": 0, "d": 16}
    pieces = {"own": zh, "down": z_down, "up": z_up, "far": lax.rem(zh + 2, NZ)}
    before = {"own": (), "down": ("u",), "up": ("d",), "far": ("u", "d")}

    def g_z1(place, way):
        if WAY[place] == "X":
            arrived(("x2", place, "u", None), ("x2", place, "d", None))
            block = gbuf.at[place, :, z_rows(zh, 0, 32)]
        else:
            block = gbuf.at[place, x, z_rows(zh, 0, 32)]
        send(("z1", place, way), block, block, to_z[way])

    def g_z2(place, way):
        arrived(("z1", place, way))
        rows = z_rows(from_z[way], kept[way], 16)
        block = gbuf.at[place, :, rows] if WAY[place] == "X" else gbuf.at[place, x, rows]
        send(("z2", place, way), block, block, to_z[way])

    def g_x1(place, way, piece=None):
        if WAY[place] == "X":
            block = gbuf.at[place, x, z_rows(zh, 0, 32)]
        elif piece is None:
            arrived(("z2", place, "u"), ("z2", place, "d"))
            block = gbuf.at[place, x]
        else:
            kind = "z2" if piece == "far" else "z1"
            arrived(*((kind, place, which) for which in before[piece]))
            block = gbuf.at[place, x, z_rows(pieces[piece], 0, 32)]
        send(("x1", place, way, piece), block, block, to_x[way])

    def g_x2(place, way, piece=None):
        arrived(("x1", place, way, piece))
        if WAY[place] == "X":
            rows = z_rows(zh, kept[way], 16)
        elif piece is None:
            rows = pl.ds(kept[way] * 4, 64)
        else:
            rows = z_rows(pieces[piece], kept[way], 16)
        block = gbuf.at[place, from_x[way], rows]
        send(("x2", place, way, piece), block, block, to_x[way])

    def g_done(place):
        for way in ("u", "d"):
            if WAY[place] == "X":
                arrived(("z2", place, way))
            elif WAY[place] == "P":
                arrived(*(("x2", place, way, piece) for piece in pieces))
            else:
                arrived(("x2", place, way, None))

    row = {"a": 2 + zl, "b": 3 - zl}

    def w_hop(block, step, way):
        if step > 1:
            arrived(("w", block, step - 1, way))
        elif block == "b":
            arrived("wz")
        relative = (1 - step) if way == "u" else (step - 1)
        source = wbuf.at[AT[relative], row[block]]
        target = wbuf.at[AT[relative - 1 if way == "u" else relative + 1], row[block]]
        send(("w", block, step, way), source, target, to_y[way])

    def w_pair():
        own = wbuf.at[AT[0], row["a"]]
        send("wz", own, own, to_pair)

    def w_core(relative):
        if relative == 0:
            arrived("wz")
        elif relative == 4:
            arrived(("w", "a", 4, "u"), ("w", "b", 4, "d"))
        else:
            way = "d" if relative > 0 else "u"
            arrived(("w", "a", abs(relative), way), ("w", "b", abs(relative), way))
        place = AT[relative]
        send(("wc", place), wbuf.at[place, 2:4], wbuf.at[place, 0:2], to_core)

    spans = (slice(0, 256), slice(256, 512))
    mine = pl.ds(pl.multiple_of(parity * 64, 64), 64)
    other = pl.ds(pl.multiple_of(64 - parity * 64, 64), 64)

    def kv_start():
        send("kv", kv_send, kv_recv, to_partner)

    def kv_ready():
        arrived("kv")
        k_turned[mine] = kv_send[0:64]
        v_turned[mine] = kv_send[64:128]
        k_turned[other] = kv_recv[0:64]
        v_turned[other] = kv_recv[64:128]
        k_full[...] = k_turned[...].astype(F32).T.astype(BF16)
        v_full[...] = v_turned[...].astype(F32).T.astype(BF16)

    def forward(head):
        columns = slice(head * 128, head * 128 + 128)
        for span in spans:
            length = span.stop
            scores = nt(k_full[0:length], q_ref[span, columns]) * scale
            key_at = lax.broadcasted_iota(jnp.int32, (length, 256), 0)
            query_at = lax.broadcasted_iota(jnp.int32, (length, 256), 1) + span.start
            scores = jnp.where(key_at <= query_at, scores, -jnp.inf)
            powers = jnp.exp(scores - jnp.max(scores, axis=0, keepdims=True))
            part = powers * (1.0 / jnp.sum(powers, axis=0, keepdims=True))
            probs[head, 0:length, span] = part
            att[columns, span] = nn(v_turned[:, 0:length], part.astype(BF16)).astype(BF16)

    def backward_values():
        for head in range(4):
            columns = slice(head * 128, head * 128 + 128)
            for span in spans[::-1]:
                length = span.stop
                part = nn(probs[head, 0:length, span].astype(BF16), grad_att[span, columns])
                if head == 0 and length == 512:
                    value_acc[...] = part
                else:
                    value_acc[0:length] += part
        value_part[...] = value_acc[...].T.astype(BF16)

    def backward_keys(at):
        span = spans[at]
        length = span.stop
        for head in range(4):
            columns = slice(head * 128, head * 128 + 128)
            part = probs[head, 0:length, span]
            dprobs = nt(v_full[0:length], grad_att[span, columns])
            delta = jnp.sum(part * dprobs, axis=0, keepdims=True)
            dscores = (part * (dprobs - delta) * scale).astype(BF16)
            gq_ref[span, columns] = nn(k_turned[:, 0:length], dscores).T.astype(BF16)
            product = nn(dscores, q_ref[span, columns])
            if head == 0 and at == 1:
                key_acc[...] = product
            else:
                key_acc[0:length] += product
        key_part[:, span] = key_acc[span].T.astype(BF16)

    def part_start(which):
        if which == 0:
            send(("part", 0), value_part.at[other], value_recv, to_partner)
        else:
            span = spans[2 - which]
            send(("part", which), key_part.at[other, span], key_recv.at[:, span], to_partner)

    def parts_done():
        arrived(("part", 0), ("part", 1), ("part", 2))
        gk_ref[...] = (key_part[mine].astype(F32) + key_recv[...].astype(F32)).astype(BF16)
        gv_ref[...] = (value_part[mine].astype(F32) + value_recv[...].astype(F32)).astype(BF16)

    summed = []

    def gather_term(place):
        g_done(place)
        arrived(("wc", place))
        for half in range(2):
            columns = slice(half * 256, half * 256 + 256)
            product = nn(
                gbuf[place].reshape(512, 512), wbuf[place, :, :, columns].reshape(512, 256)
            )
            if not summed:
                total[:, columns] = product
            elif len(summed) < 7:
                total[:, columns] += product
            else:
                grad_att[:, columns] = (total[:, columns] + product).astype(BF16)
        summed.append(place)

    def weight_term(place):
        g_done(place)
        features = gbuf[place].reshape(512, 512)
        product = nn(att[...], features[:, 0:256])
        core_send[place, 0] = product[:, 0:128].astype(BF16)
        core_send[place, 1] = product[:, 128:256].astype(BF16)

    def core_start(place):
        send(("core", place), core_send.at[place], core_recv.at[place], to_core)
        features = gbuf[place].reshape(512, 512)
        product = nn(att[...], features[:, 256:512])
        terms[place, 0] = product[:, 0:128]
        terms[place, 1] = product[:, 128:256]

    at_of = {"a": zl, "b": 1 - zl}

    def ring(block, place):
        relative = ORDER[place]
        at = at_of[block]
        arrived(("core", place))
        partial = terms[place, at] + core_recv[place, at].astype(F32)
        if relative != 4 and (relative, block) not in ((3, "b"), (-3, "a")):
            if relative >= 0:
                arrived(("ring", block, relative + 1, "u"))
                partial += y_recv[place, at].astype(F32)
            if relative <= 0:
                arrived(("ring", block, relative - 1, "d"))
                slot = ABOVE if relative == 0 else place
                partial += y_recv[slot, at].astype(F32)
        if relative:
            y_send[place, at] = partial.astype(BF16)
        elif block == "b":
            z_send[...] = partial.astype(BF16)
        else:
            terms[place, at] = partial

    def ring_start(block, place):
        relative = ORDER[place]
        at = at_of[block]
        up = block == "a" if relative == 4 else relative > 0
        if up:
            relative, slot, way = relative, AT[relative - 1], "u"
        else:
            relative = -abs(relative)
            slot, way = ABOVE if relative == -1 else AT[relative + 1], "d"
        send(("ring", block, relative, way), y_send.at[place, at], y_recv.at[slot, at], to_y[way])

    def pair_start():
        send("pair", z_send, z_recv, to_pair)

    def ring_done():
        arrived("pair")
        gw_ref[...] = (terms[AT[0], zl] + z_recv[...].astype(F32)).T.astype(BF16)

    g_x1(0, "d", "own")
    g_x1(0, "u", "own")
    g_x1(1, "d", "own")
    g_x1(1, "u", "own")
    g_z1(0, "d")
    g_z1(0, "u")
    g_z1(1, "d")
    g_z1(1, "u")
    w_hop("a", 1, "d")
    w_hop("a", 1, "u")
    g_x1(2, "d", "own")
    g_x1(2, "u", "own")
    g_x1(3, "d", "own")
    g_x1(3, "u", "own")
    g_z1(2, "d")
    w_pair()
    g_x1(4, "d", "own")
    g_x1(4, "u", "own")
    g_x1(5, "d", "own")
    g_x1(5, "u", "own")
    g_z1(3, "d")
    g_z1(2, "u")
    g_x2(0, "d", "own")
    g_x2(0, "u", "own")
    g_x2(1, "d", "own")
    g_x2(1, "u", "own")
    g_z1(4, "d")
    g_x2(2, "d", "own")
    g_x2(2, "u", "own")
    g_x2(3, "d", "own")
    g_x2(3, "u", "own")
    w_hop("a", 2, "d")
    g_x1(0, "d", "up")
    g_x1(0, "u", "down")
    w_hop("a", 2, "u")
    g_x1(0, "d", "down")
    g_x1(0, "u", "up")
    g_z2(0, "d")
    g_z2(0, "u")
    g_x2(4, "d", "own")
    g_x2(4, "u", "own")
    g_x1(1, "d", "down")
    g_x1(1, "u", "down")
    g_x1(1, "d", "up")
    g_x1(1, "u", "up")
    g_z2(1, "d")
    g_z2(1, "u")
    g_x2(5, "d", "own")
    g_x2(5, "u", "own")
    g_z1(5, "d")
    g_z1(3, "u")
    g_x1(2, "d", "up")
    g_x1(2, "u", "up")
    g_z2(2, "d")
    g_z1(4, "u")
    g_x2(0, "d", "up")
    g_x2(0, "u", "down")
    g_x2(0, "d", "down")
    g_x2(0, "u", "up")
    w_hop("b", 1, "d")
    w_hop("b", 1, "u")
    g_x1(3, "d", "up")
    g_x1(3, "u", "up")
    w_core(0)
    g_z2(3, "d")
    kv_start()
    w_hop("a", 3, "d")
    w_hop("a", 3, "u")
    g_x2(1, "d", "down")
    g_x2(1, "u", "down")
    g_z1(6, "d")
    g_x1(4, "d", "up")
    g_x1(2, "d", "down")
    g_x1(2, "u", "down")
    g_x1(4, "u", "up")
    g_z2(4, "d")
    g_z2(2, "u")
    g_x2(1, "d", "up")
    g_x2(1, "u", "up")
    g_x1(0, "d", "far")
    g_x1(0, "u", "far")
    g_x1(1, "d", "far")
    g_x1(1, "u", "far")
    g_z1(7, "d")
    g_x2(2, "d", "up")
    g_x2(2, "u", "up")
    g_z2(5, "d")
    g_x2(3, "d", "up")
    g_x2(3, "u", "up")
    g_x1(3, "d", "down")
    g_x1(3, "u", "down")
    g_z2(3, "u")
    g_x2(4, "d", "up")
    g_x2(2, "u", "down")
    w_hop("b", 2, "d")
    w_hop("b", 2, "u")
    w_core(1)
    w_core(-1)
    g_z1(5, "u")
    g_x2(2, "d", "down")
    g_x2(4, "u", "up")
    g_x1(4, "d", "down")
    g_x1(4, "u", "down")
    g_x1(5, "d", "up")
    g_x1(5, "u", "up")
    g_z2(4, "u")
    g_x2(0, "d", "far")
    g_x2(0, "u", "far")
    g_z2(6, "d")
    g_x2(1, "d", "far")
    g_x2(1, "u", "far")
    w_hop("a", 4, "u")
    g_z1(6, "u")
    g_x2(3, "d", "down")
    g_x2(3, "u", "down")
    g_z1(7, "u")
    kv_ready()
    forward(0)
    g_z2(7, "d")
    g_x1(2, "d", "far")
    g_x1(2, "u", "far")
    forward(1)
    g_x2(4, "d", "down")
    g_x2(4, "u", "down")
    forward(2)
    g_x1(3, "d", "far")
    g_x1(3, "u", "far")
    w_hop("b", 3, "d")
    w_hop("b", 3, "u")
    g_x2(5, "d", "up")
    g_x2(5, "u", "up")
    w_core(2)
    w_core(-2)
    forward(3)
    weight_term(0)
    core_start(0)
    g_z2(5, "u")
    g_x1(5, "d", "down")
    g_x1(5, "u", "down")
    weight_term(1)
    core_start(1)
    g_x1(4, "d", "far")
    g_x1(4, "u", "far")
    g_x2(2, "d", "far")
    g_x2(2, "u", "far")
    g_z2(6, "u")
    g_x2(3, "d", "far")
    g_x2(3, "u", "far")
    ring("a", 0)
    ring_start("a", 0)
    ring("b", 0)
    ring_start("b", 0)
    ring("b", 1)
    ring_start("b", 1)
    g_z2(7, "u")
    g_x2(5, "d", "down")
    g_x2(5, "u", "down")
    w_hop("b", 4, "d")
    w_core(3)
    w_core(-3)
    g_x2(4, "d", "far")
    g_x2(4, "u", "far")
    weight_term(2)
    core_start(2)
    g_x1(5, "d", "far")
    g_x1(5, "u", "far")
    weight_term(3)
    core_start(3)
    gather_term(1)
    gather_term(3)
    g_x1(6, "d")
    g_x1(6, "u")
    gather_term(2)
    weight_term(4)
    core_start(4)
    ring("a", 2)
    ring_start("a", 2)
    ring("a", 1)
    ring_start("a", 1)
    ring("b", 2)
    g_x1(7, "d")
    g_x1(7, "u")
    ring_start("b", 2)
    gather_term(4)
    g_x2(5, "d", "far")
    g_x2(5, "u", "far")
    ring("b", 3)
    ring_start("b", 3)
    w_core(4)
    g_x2(6, "d")
    g_x2(6, "u")
    gather_term(0)
    ring("a", 4)
    ring_start("a", 4)
    ring("a", 3)
    ring_start("a", 3)
    g_x2(7, "d")
    g_x2(7, "u")
    weight_term(5)
    core_start(5)
    gather_term(5)
    ring("b", 4)
    ring_start("b", 4)
    weight_term(6)
    core_start(6)
    gather_term(6)
    ring("b", 5)
    ring_start("b", 5)
    ring("a", 6)
    ring_start("a", 6)
    ring("a", 5)
    ring_start("a", 5)
    gather_term(7)
    weight_term(7)
    core_start(7)
    backward_values()
    part_start(0)
    backward_keys(1)
    part_start(1)
    ring("b", 6)
    ring_start("b", 6)
    backward_keys(0)
    part_start(2)
    ring("a", 7)
    ring("b", 7)
    pair_start()
    parts_done()
    ring_done()
    for copy in copies.values():
        copy.wait_send()


def body(queries, keys, values, grad_out, out_weight):
    vmem = pl.BlockSpec(memory_space=pltpu.VMEM)
    grad_q, grad_k, grad_v, grad_weight = pl.pallas_call(
        kernel,
        out_shape=(
            jax.ShapeDtypeStruct((512, 512), BF16),
            jax.ShapeDtypeStruct((64, 512), BF16),
            jax.ShapeDtypeStruct((64, 512), BF16),
            jax.ShapeDtypeStruct((128, 512), BF16),
        ),
        in_specs=[vmem] * 5,
        out_specs=(vmem,) * 4,
        scratch_shapes=[
            pltpu.VMEM((8, 4, 128, 512), BF16),
            pltpu.VMEM((8, 4, 128, 512), BF16),
            pltpu.VMEM((128, 512), BF16),
            pltpu.VMEM((128, 512), BF16),
            pltpu.VMEM((512, 128), BF16),
            pltpu.VMEM((512, 128), BF16),
            pltpu.VMEM((128, 512), BF16),
            pltpu.VMEM((128, 512), BF16),
            pltpu.VMEM((4, 512, 512), F32),
            pltpu.VMEM((512, 512), BF16),
            pltpu.VMEM((512, 512), F32),
            pltpu.VMEM((512, 512), BF16),
            pltpu.VMEM((8, 2, 512, 128), F32),
            pltpu.VMEM((8, 2, 512, 128), BF16),
            pltpu.VMEM((8, 2, 512, 128), BF16),
            pltpu.VMEM((8, 2, 512, 128), BF16),
            pltpu.VMEM((9, 2, 512, 128), BF16),
            pltpu.VMEM((512, 128), BF16),
            pltpu.VMEM((512, 128), BF16),
            pltpu.VMEM((512, 128), F32),
            pltpu.VMEM((512, 128), F32),
            pltpu.VMEM((128, 512), BF16),
            pltpu.VMEM((128, 512), BF16),
            pltpu.VMEM((64, 512), BF16),
            pltpu.VMEM((64, 512), BF16),
            pltpu.SemaphoreType.DMA((N_COPIES,)),
            pltpu.SemaphoreType.DMA((N_COPIES,)),
        ],
        compiler_params=pltpu.CompilerParams(
            collective_id=0, has_side_effects=True, vmem_limit_bytes=56 * 1024 * 1024
        ),
        cost_estimate=pl.CostEstimate(
            flops=6_000_000_000, bytes_accessed=4_000_000, transcendentals=1_000_000
        ),
    )(queries, keys.T, values.T, grad_out, out_weight)
    return grad_q, grad_k.T, grad_v.T, grad_weight


def solution(mesh):
    placed = (
        P("dp", "tensor"),
        P("dp", "tensor"),
        P("dp", "tensor"),
        P(("dp", "tensor"), None),
        P("dp", "tensor"),
    )
    return jax.shard_map(
        body,
        mesh=mesh,
        in_specs=placed,
        out_specs=(P("dp", "tensor"), P("dp", "tensor"), P("dp", "tensor"), P("dp", "tensor")),
        check_vma=False,
    )
```

time: 106 us -> 82.2 us (0.78)
  the two profiles are of different devices: /device:TPU:25 before, /device:TPU:88 now
where the time goes in v2:
time: 82.2 us; the launch traced here: 82 us
  Pallas kernels  77.6 us (94%)
  local copies, waits for them, and re-layouts  3.83 us (5%)
    pallas_call x1, Pallas kernels, body(): pl.pallas_call(kernel, out_shape=(jax.ShapeDtypeStruct((512, 512), BF16),...  77.6 us
    unnamed x10, local copies, waits for them, and re-layouts  3.83 us

profile of v2, /device:TPU:88, one launch (start us, length us, event | category | flops | bytes accessed | tf_op | source)
XLA Modules:
  0.0 82.0 jit_solution(7069170000242556900)
XLA Ops:
  0.6 77.6 %shard_map.84 = (bf16[512,512]{1,0:T(8,128)(2,1)}, bf16[64,512]{1,0:T(8,128)(2,1)}, bf16[64,512]{1,0:T(8,128)(2,1)}, bf16[128,512]{1,0:T(8,128)(2,1)}) custom-call(bf16[512,512]{1,0:T(8,128)(2,1)} %q_ref.1, bf16[64,512]{1,0:T(8,128)(2,1)} %bitcast.6, bf16[64,512]{1,0:T(8,128)(2,1)} %bitcast.7, bf16[32,4096]{1,0:T(8,128)(2,1)} %g_ref.1, bf16[128,512]{1,0:T(8,128)(2,1)} %w_ref.1), custom_call_target="tpu_custom_call" | custom-call | flops 6000000000 | bytes 4000000 | tf_op jit(solution)/shard_map/pallas_call | solution.py:559
  78.2 0.0 copy-start.2
  78.2 0.0 copy-start.1
  78.2 1.9 %copy.13 = bf16[512,512]{1,0:T(8,128)(2,1)} copy(bf16[512,512]{1,0:T(8,128)(2,1)} %get-tuple-element.16) | data formatting | bytes 1048576
  80.1 0.0 copy-done.2
  80.1 0.0 copy-start
  80.1 0.6 copy.14
  80.7 0.0 copy-done.1
  80.8 0.6 copy.15
  81.4 0.0 copy-done
  81.4 0.7 copy.16
Async XLA Ops:
  78.2 1.9 %copy-start.2 = (bf16[64,512]{1,0:T(8,128)(2,1)S(1)}, bf16[64,512]{1,0:T(8,128)(2,1)}, u32[]{:S(2)}) copy-start(bf16[64,512]{1,0:T(8,128)(2,1)} %get-tuple-element.9) | copy-start | bytes 196612
  78.2 2.5 %copy-start.1 = (bf16[64,512]{1,0:T(8,128)(2,1)S(1)}, bf16[64,512]{1,0:T(8,128)(2,1)}, u32[]{:S(2)}) copy-start(bf16[64,512]{1,0:T(8,128)(2,1)} %get-tuple-element.10) | copy-start | bytes 196612
  80.1 1.3 %copy-start = (bf16[128,512]{1,0:T(8,128)(2,1)S(1)}, bf16[128,512]{1,0:T(8,128)(2,1)}, u32[]{:S(2)}) copy-start(bf16[128,512]{1,0:T(8,128)(2,1)} %get-tuple-element.19) | copy-start | bytes 393220

commit v3 on v2

--- a/solution.py
+++ b/solution.py
@@ -16,7 +16,9 @@
 ABOVE = 8
 
 NX, NZ, NY = 4, 4, 8
-N_COPIES = 208
+N_COPIES = 224
+
+PAIR, W_PAIR = 4, 5
 
 WAY = tuple('PPPPPPZZ')
 
@@ -30,8 +32,9 @@
 
 
 def kernel(
-    q_ref, k_ref, v_ref, g_ref, w_ref,
-    gq_ref, gk_ref, gv_ref, gw_ref,
+    q_in, k_in, v_in, g_in, w_in,
+    gq_out, gk_out, gv_out, gw_out,
+    q_ref, g_ref, gq_ref, gk_ref, gv_ref, gw_ref, local_sem,
     gbuf, wbuf, kv_send, kv_recv, k_full, v_full, k_turned, v_turned,
     probs, att, total, grad_att, terms, core_send, core_recv, y_send, y_recv,
     z_send, z_recv, key_acc, value_acc, key_part, value_part, key_recv, value_recv, send_sem, recv_sem,
@@ -82,9 +85,23 @@
                 copies[name].wait_recv()
                 waited.add(name)
 
-    kv_send[0:64] = k_ref[...]
-    kv_send[64:128] = v_ref[...]
-    wbuf[AT[0], 2 + zl] = w_ref[...]
+    loads = [
+        pltpu.make_async_copy(source, target, local_sem.at[i])
+        for i, (source, target) in enumerate((
+            (g_in, g_ref), (k_in, kv_send.at[0:64]), (v_in, kv_send.at[64:128]),
+            (w_in, wbuf.at[AT[0], 2 + zl]), (q_in, q_ref),
+        ))
+    ]
+    for load in loads:
+        load.start()
+    stores = []
+
+    def store(source, target):
+        copy = pltpu.make_async_copy(source, target, local_sem.at[len(loads) + len(stores)])
+        copy.start()
+        stores.append(copy)
+
+    loads[0].wait()
     own_rows = pl.ds(pl.multiple_of(zh * 32, 32), 32)
     for place, relative in enumerate(ORDER):
         column = lax.rem(y + relative + NY, NY)
@@ -94,6 +111,8 @@
             gbuf[place, x, own_rows, slot * 128 : (slot + 1) * 128] = g_ref[
                 :, pl.ds(pl.multiple_of(block * 128, 128), 128)
             ]
+    for load in loads[1:4]:
+        load.wait()
     pl.semaphore_wait(barrier, 8)
 
     def z_rows(at, first, count):
@@ -159,24 +178,35 @@
         if step > 1:
             arrived(("w", block, step - 1, way))
         elif block == "b":
-            arrived("wz")
+            arrived(("wz", AT[0]))
         relative = (1 - step) if way == "u" else (step - 1)
         source = wbuf.at[AT[relative], row[block]]
         target = wbuf.at[AT[relative - 1 if way == "u" else relative + 1], row[block]]
+        if step == 4 and W_PAIR <= 4:
+            rows = slice(0, 64) if way == "u" else slice(64, 128)
+            source, target = source.at[rows], target.at[rows]
         send(("w", block, step, way), source, target, to_y[way])
 
-    def w_pair():
-        own = wbuf.at[AT[0], row["a"]]
-        send("wz", own, own, to_pair)
+    def w_arrived(block, relative):
+        far = abs(relative)
+        if block == "b" and (relative == 0 or far >= W_PAIR):
+            arrived(("wz", AT[relative]))
+        elif far == 4 and W_PAIR <= 4:
+            arrived(("w", block, 4, "u"), ("w", block, 4, "d"))
+        elif far == 4:
+            arrived(("w", block, 4, "u" if block == "a" else "d"))
+        elif far:
+            arrived(("w", block, far, "d" if relative > 0 else "u"))
+
+    def w_pair(relative):
+        w_arrived("a", relative)
+        place = AT[relative]
+        block = wbuf.at[place, row["a"]]
+        send(("wz", place), block, block, to_pair)
 
     def w_core(relative):
-        if relative == 0:
-            arrived("wz")
-        elif relative == 4:
-            arrived(("w", "a", 4, "u"), ("w", "b", 4, "d"))
-        else:
-            way = "d" if relative > 0 else "u"
-            arrived(("w", "a", abs(relative), way), ("w", "b", abs(relative), way))
+        w_arrived("a", relative)
+        w_arrived("b", relative)
         place = AT[relative]
         send(("wc", place), wbuf.at[place, 2:4], wbuf.at[place, 0:2], to_core)
 
@@ -189,6 +219,7 @@
 
     def kv_ready():
         arrived("kv")
+        loads[4].wait()
         k_turned[mine] = kv_send[0:64]
         v_turned[mine] = kv_send[64:128]
         k_turned[other] = kv_recv[0:64]
@@ -237,6 +268,7 @@
             else:
                 key_acc[0:length] += product
         key_part[:, span] = key_acc[span].T.astype(BF16)
+        store(gq_ref.at[span], gq_out.at[span])
 
     def part_start(which):
         if which == 0:
@@ -249,6 +281,8 @@
         arrived(("part", 0), ("part", 1), ("part", 2))
         gk_ref[...] = (key_part[mine].astype(F32) + key_recv[...].astype(F32)).astype(BF16)
         gv_ref[...] = (value_part[mine].astype(F32) + value_recv[...].astype(F32)).astype(BF16)
+        store(gk_ref, gk_out)
+        store(gv_ref, gv_out)
 
     summed = []
 
@@ -286,41 +320,60 @@
 
     def ring(block, place):
         relative = ORDER[place]
+        far = abs(relative)
         at = at_of[block]
         arrived(("core", place))
         partial = terms[place, at] + core_recv[place, at].astype(F32)
-        if relative != 4 and (relative, block) not in ((3, "b"), (-3, "a")):
-            if relative >= 0:
-                arrived(("ring", block, relative + 1, "u"))
-                partial += y_recv[place, at].astype(F32)
-            if relative <= 0:
-                arrived(("ring", block, relative - 1, "d"))
-                slot = ABOVE if relative == 0 else place
-                partial += y_recv[slot, at].astype(F32)
+        if block == "a" and relative and far >= PAIR:
+            arrived(("pair", place))
+            partial += z_recv[place].astype(F32)
         if relative:
             y_send[place, at] = partial.astype(BF16)
-        elif block == "b":
-            z_send[...] = partial.astype(BF16)
+        for way, sign in (("u", 1), ("d", -1)):
+            if relative * sign < 0 or relative == 4:
+                continue
+            rows, slot = slice(0, 512), ABOVE if relative == 0 and way == "d" else place
+            if far == 3 and PAIR <= 4:
+                rows = slice(0, 256) if way == "u" else slice(256, 512)
+                comes = block == "a"
+            elif far == 3:
+                comes = block == ("a" if way == "u" else "b")
+            else:
+                comes = block == "a" or far + 1 < PAIR
+            if not comes:
+                continue
+            arrived(("ring", block, sign * (far + 1), way))
+            if far == 3 and PAIR <= 4:
+                y_send[place, at, rows] = (partial[rows] + y_recv[slot, at, rows].astype(F32)).astype(BF16)
+            else:
+                partial += y_recv[slot, at].astype(F32)
+                if relative:
+                    y_send[place, at] = partial.astype(BF16)
+        if block == "b" and (relative == 0 or far >= PAIR):
+            z_send[place] = partial.astype(BF16)
+        elif relative == 0:
+            terms[place, at] = partial
+
+    def ring_start(block, place, way):
+        relative = -4 if ORDER[place] == 4 and way == "d" else ORDER[place]
+        at = at_of[block]
+        rows = slice(0, 512)
+        if relative in (4, -4) and PAIR <= 4:
+            rows = slice(0, 256) if way == "u" else slice(256, 512)
+        if way == "u":
+            slot = AT[relative - 1]
         else:
-            terms[place, at] = partial
-
-    def ring_start(block, place):
-        relative = ORDER[place]
-        at = at_of[block]
-        up = block == "a" if relative == 4 else relative > 0
-        if up:
-            relative, slot, way = relative, AT[relative - 1], "u"
-        else:
-            relative = -abs(relative)
-            slot, way = ABOVE if relative == -1 else AT[relative + 1], "d"
-        send(("ring", block, relative, way), y_send.at[place, at], y_recv.at[slot, at], to_y[way])
-
-    def pair_start():
-        send("pair", z_send, z_recv, to_pair)
+            slot = ABOVE if relative == -1 else AT[relative + 1]
+        send(("ring", block, relative, way), y_send.at[place, at, rows], y_recv.at[slot, at, rows], to_y[way])
+
+    def pair_start(place):
+        send(("pair", place), z_send.at[place], z_recv.at[place], to_pair)
 
     def ring_done():
-        arrived("pair")
-        gw_ref[...] = (terms[AT[0], zl] + z_recv[...].astype(F32)).T.astype(BF16)
+        place = AT[0]
+        arrived(("pair", place))
+        gw_ref[...] = (terms[place, zl] + z_recv[place].astype(F32)).T.astype(BF16)
+        store(gw_ref, gw_out)
 
     g_x1(0, "d", "own")
     g_x1(0, "u", "own")
@@ -328,8 +381,8 @@
     g_x1(1, "u", "own")
     g_z1(0, "d")
     g_z1(0, "u")
+    w_pair(0)
     g_z1(1, "d")
-    g_z1(1, "u")
     w_hop("a", 1, "d")
     w_hop("a", 1, "u")
     g_x1(2, "d", "own")
@@ -337,225 +390,234 @@
     g_x1(3, "d", "own")
     g_x1(3, "u", "own")
     g_z1(2, "d")
-    w_pair()
+    kv_start()
     g_x1(4, "d", "own")
     g_x1(4, "u", "own")
     g_x1(5, "d", "own")
     g_x1(5, "u", "own")
     g_z1(3, "d")
-    g_z1(2, "u")
     g_x2(0, "d", "own")
     g_x2(0, "u", "own")
     g_x2(1, "d", "own")
     g_x2(1, "u", "own")
     g_z1(4, "d")
+    g_z1(1, "u")
     g_x2(2, "d", "own")
     g_x2(2, "u", "own")
     g_x2(3, "d", "own")
-    g_x2(3, "u", "own")
     w_hop("a", 2, "d")
+    w_hop("a", 2, "u")
     g_x1(0, "d", "up")
     g_x1(0, "u", "down")
-    w_hop("a", 2, "u")
+    g_x1(0, "u", "up")
     g_x1(0, "d", "down")
-    g_x1(0, "u", "up")
     g_z2(0, "d")
-    g_z2(0, "u")
+    g_x2(3, "u", "own")
     g_x2(4, "d", "own")
     g_x2(4, "u", "own")
-    g_x1(1, "d", "down")
-    g_x1(1, "u", "down")
     g_x1(1, "d", "up")
+    w_hop("b", 1, "d")
+    w_hop("b", 1, "u")
+    w_core(0)
     g_x1(1, "u", "up")
+    g_x2(5, "d", "own")
     g_z2(1, "d")
-    g_z2(1, "u")
-    g_x2(5, "d", "own")
+    g_z2(0, "u")
     g_x2(5, "u", "own")
     g_z1(5, "d")
-    g_z1(3, "u")
     g_x1(2, "d", "up")
     g_x1(2, "u", "up")
     g_z2(2, "d")
-    g_z1(4, "u")
+    g_x2(0, "u", "down")
+    g_z1(2, "u")
     g_x2(0, "d", "up")
-    g_x2(0, "u", "down")
+    g_x2(0, "u", "up")
+    g_z1(3, "u")
     g_x2(0, "d", "down")
-    g_x2(0, "u", "up")
-    w_hop("b", 1, "d")
-    w_hop("b", 1, "u")
     g_x1(3, "d", "up")
     g_x1(3, "u", "up")
-    w_core(0)
     g_z2(3, "d")
-    kv_start()
     w_hop("a", 3, "d")
     w_hop("a", 3, "u")
+    g_x2(1, "d", "up")
+    g_x2(1, "u", "up")
+    g_z1(6, "d")
+    g_z1(4, "u")
+    g_x1(4, "d", "up")
+    g_x1(4, "u", "up")
+    kv_ready()
+    forward(0)
+    g_z2(4, "d")
+    g_x2(2, "d", "up")
+    g_x2(2, "u", "up")
+    forward(1)
+    g_z1(5, "u")
+    g_x1(1, "d", "down")
+    g_x1(1, "u", "down")
+    forward(2)
+    w_hop("b", 2, "d")
+    w_hop("b", 2, "u")
+    g_x2(3, "u", "up")
+    w_core(1)
+    w_core(-1)
+    g_x1(0, "d", "far")
+    g_x1(0, "u", "far")
+    g_x2(3, "d", "up")
+    g_z1(7, "d")
+    forward(3)
+    g_z2(1, "u")
+    g_z2(5, "d")
+    g_x1(5, "d", "up")
+    g_x1(5, "u", "up")
+    g_x2(4, "d", "up")
+    g_x2(4, "u", "up")
+    g_x1(2, "u", "down")
+    g_x1(2, "d", "down")
+    g_z2(2, "u")
+    w_hop("a", 4, "u")
+    g_z1(6, "u")
     g_x2(1, "d", "down")
     g_x2(1, "u", "down")
-    g_z1(6, "d")
-    g_x1(4, "d", "up")
-    g_x1(2, "d", "down")
-    g_x1(2, "u", "down")
-    g_x1(4, "u", "up")
-    g_z2(4, "d")
-    g_z2(2, "u")
-    g_x2(1, "d", "up")
-    g_x2(1, "u", "up")
-    g_x1(0, "d", "far")
-    g_x1(0, "u", "far")
-    g_x1(1, "d", "far")
-    g_x1(1, "u", "far")
-    g_z1(7, "d")
-    g_x2(2, "d", "up")
-    g_x2(2, "u", "up")
-    g_z2(5, "d")
-    g_x2(3, "d", "up")
-    g_x2(3, "u", "up")
     g_x1(3, "d", "down")
     g_x1(3, "u", "down")
     g_z2(3, "u")
-    g_x2(4, "d", "up")
-    g_x2(2, "u", "down")
-    w_hop("b", 2, "d")
-    w_hop("b", 2, "u")
-    w_core(1)
-    w_core(-1)
-    g_z1(5, "u")
-    g_x2(2, "d", "down")
-    g_x2(4, "u", "up")
+    g_x2(0, "d", "far")
+    g_z2(6, "d")
+    g_x2(0, "u", "far")
     g_x1(4, "d", "down")
     g_x1(4, "u", "down")
-    g_x1(5, "d", "up")
-    g_x1(5, "u", "up")
+    g_x2(5, "d", "up")
+    g_x2(5, "u", "up")
     g_z2(4, "u")
-    g_x2(0, "d", "far")
-    g_x2(0, "u", "far")
-    g_z2(6, "d")
-    g_x2(1, "d", "far")
-    g_x2(1, "u", "far")
-    w_hop("a", 4, "u")
-    g_z1(6, "u")
+    w_hop("b", 3, "d")
+    w_hop("b", 3, "u")
+    w_core(2)
+    w_core(-2)
+    g_x2(2, "u", "down")
+    g_x2(2, "d", "down")
+    g_z1(7, "u")
+    g_z2(7, "d")
+    g_x1(5, "d", "down")
+    g_x1(5, "u", "down")
+    g_z2(5, "u")
     g_x2(3, "d", "down")
+    g_x1(1, "d", "far")
+    g_x1(1, "u", "far")
     g_x2(3, "u", "down")
-    g_z1(7, "u")
-    kv_ready()
-    forward(0)
-    g_z2(7, "d")
+    weight_term(0)
+    core_start(0)
     g_x1(2, "d", "far")
     g_x1(2, "u", "far")
-    forward(1)
     g_x2(4, "d", "down")
     g_x2(4, "u", "down")
-    forward(2)
+    g_z2(6, "u")
+    ring("b", 0)
+    pair_start(0)
+    g_x2(5, "d", "down")
+    g_x2(5, "u", "down")
     g_x1(3, "d", "far")
     g_x1(3, "u", "far")
-    w_hop("b", 3, "d")
-    w_hop("b", 3, "u")
-    g_x2(5, "d", "up")
-    g_x2(5, "u", "up")
-    w_core(2)
-    w_core(-2)
-    forward(3)
-    weight_term(0)
-    core_start(0)
-    g_z2(5, "u")
-    g_x1(5, "d", "down")
-    g_x1(5, "u", "down")
-    weight_term(1)
-    core_start(1)
+    w_hop("b", 4, "d")
+    g_x2(1, "u", "far")
+    w_core(3)
+    w_core(-3)
     g_x1(4, "d", "far")
+    g_x2(1, "d", "far")
     g_x1(4, "u", "far")
     g_x2(2, "d", "far")
     g_x2(2, "u", "far")
-    g_z2(6, "u")
+    g_z2(7, "u")
+    g_x1(5, "d", "far")
+    g_x1(5, "u", "far")
     g_x2(3, "d", "far")
     g_x2(3, "u", "far")
-    ring("a", 0)
-    ring_start("a", 0)
-    ring("b", 0)
-    ring_start("b", 0)
-    ring("b", 1)
-    ring_start("b", 1)
-    g_z2(7, "u")
-    g_x2(5, "d", "down")
-    g_x2(5, "u", "down")
-    w_hop("b", 4, "d")
-    w_core(3)
-    w_core(-3)
+    g_x1(6, "d")
+    g_x1(6, "u")
     g_x2(4, "d", "far")
+    weight_term(1)
+    core_start(1)
     g_x2(4, "u", "far")
     weight_term(2)
     core_start(2)
-    g_x1(5, "d", "far")
-    g_x1(5, "u", "far")
+    gather_term(1)
+    ring("a", 0)
+    ring_start("a", 0, "d")
+    ring_start("a", 0, "u")
+    w_core(4)
+    gather_term(2)
+    g_x2(5, "d", "far")
+    g_x2(5, "u", "far")
+    ring("b", 1)
+    ring_start("b", 1, "u")
     weight_term(3)
     core_start(3)
-    gather_term(1)
     gather_term(3)
-    g_x1(6, "d")
-    g_x1(6, "u")
-    gather_term(2)
+    ring("b", 2)
+    ring_start("b", 2, "d")
+    g_x1(7, "d")
+    g_x1(7, "u")
+    gather_term(0)
+    g_x2(6, "d")
+    g_x2(6, "u")
+    ring("a", 2)
+    ring_start("a", 2, "d")
+    ring("a", 1)
+    ring_start("a", 1, "u")
     weight_term(4)
     core_start(4)
-    ring("a", 2)
-    ring_start("a", 2)
-    ring("a", 1)
-    ring_start("a", 1)
-    ring("b", 2)
-    g_x1(7, "d")
-    g_x1(7, "u")
-    ring_start("b", 2)
+    weight_term(5)
+    core_start(5)
     gather_term(4)
-    g_x2(5, "d", "far")
-    g_x2(5, "u", "far")
+    gather_term(5)
     ring("b", 3)
-    ring_start("b", 3)
-    w_core(4)
-    g_x2(6, "d")
-    g_x2(6, "u")
-    gather_term(0)
-    ring("a", 4)
-    ring_start("a", 4)
-    ring("a", 3)
-    ring_start("a", 3)
+    ring_start("b", 3, "u")
+    ring("b", 4)
+    ring_start("b", 4, "d")
     g_x2(7, "d")
     g_x2(7, "u")
-    weight_term(5)
-    core_start(5)
-    gather_term(5)
-    ring("b", 4)
-    ring_start("b", 4)
     weight_term(6)
     core_start(6)
     gather_term(6)
-    ring("b", 5)
-    ring_start("b", 5)
-    ring("a", 6)
-    ring_start("a", 6)
-    ring("a", 5)
-    ring_start("a", 5)
+    ring("a", 3)
+    ring_start("a", 3, "u")
+    ring("a", 4)
+    ring_start("a", 4, "d")
     gather_term(7)
     weight_term(7)
     core_start(7)
+    ring("b", 5)
+    ring_start("b", 5, "u")
+    ring("b", 6)
+    ring_start("b", 6, "d")
     backward_values()
     part_start(0)
     backward_keys(1)
     part_start(1)
-    ring("b", 6)
-    ring_start("b", 6)
     backward_keys(0)
     part_start(2)
+    ring("a", 5)
+    ring_start("a", 5, "u")
+    ring("a", 6)
+    ring_start("a", 6, "d")
+    ring("b", 7)
+    pair_start(7)
+    parts_done()
     ring("a", 7)
-    ring("b", 7)
-    pair_start()
-    parts_done()
     ring_done()
     for copy in copies.values():
         copy.wait_send()
+    for copy in stores:
+        copy.wait()
+
+
+def place_results(*refs):
+    for i in range(4):
+        refs[i + 4][...] = refs[i][...]
 
 
 def body(queries, keys, values, grad_out, out_weight):
     vmem = pl.BlockSpec(memory_space=pltpu.VMEM)
+    anywhere = pl.BlockSpec(memory_space=pl.ANY)
     grad_q, grad_k, grad_v, grad_weight = pl.pallas_call(
         kernel,
         out_shape=(
@@ -564,9 +626,16 @@
             jax.ShapeDtypeStruct((64, 512), BF16),
             jax.ShapeDtypeStruct((128, 512), BF16),
         ),
-        in_specs=[vmem] * 5,
-        out_specs=(vmem,) * 4,
+        in_specs=[anywhere] * 5,
+        out_specs=(anywhere,) * 4,
         scratch_shapes=[
+            pltpu.VMEM((512, 512), BF16),
+            pltpu.VMEM((32, 4096), BF16),
+            pltpu.VMEM((512, 512), BF16),
+            pltpu.VMEM((64, 512), BF16),
+            pltpu.VMEM((64, 512), BF16),
+            pltpu.VMEM((128, 512), BF16),
+            pltpu.SemaphoreType.DMA((10,)),
             pltpu.VMEM((8, 4, 128, 512), BF16),
             pltpu.VMEM((8, 4, 128, 512), BF16),
             pltpu.VMEM((128, 512), BF16),
@@ -584,8 +653,8 @@
             pltpu.VMEM((8, 2, 512, 128), BF16),
             pltpu.VMEM((8, 2, 512, 128), BF16),
             pltpu.VMEM((9, 2, 512, 128), BF16),
-            pltpu.VMEM((512, 128), BF16),
-            pltpu.VMEM((512, 128), BF16),
+            pltpu.VMEM((8, 512, 128), BF16),
+            pltpu.VMEM((8, 512, 128), BF16),
             pltpu.VMEM((512, 128), F32),
             pltpu.VMEM((512, 128), F32),
             pltpu.VMEM((128, 512), BF16),
@@ -602,6 +671,14 @@
             flops=6_000_000_000, bytes_accessed=4_000_000, transcendentals=1_000_000
         ),
     )(queries, keys.T, values.T, grad_out, out_weight)
+    results = (grad_q, grad_k, grad_v, grad_weight)
+    grad_q, grad_k, grad_v, grad_weight = pl.pallas_call(
+        place_results,
+        out_shape=tuple(jax.ShapeDtypeStruct(array.shape, array.dtype) for array in results),
+        in_specs=[vmem] * 4,
+        out_specs=(vmem,) * 4,
+        cost_estimate=pl.CostEstimate(flops=0, bytes_accessed=1_600_000, transcendentals=0),
+    )(*results)
     return grad_q, grad_k.T, grad_v.T, grad_weight
 
 

time: 82.2 us -> 77 us (0.937)
  the two profiles are of different devices: /device:TPU:88 before, /device:TPU:136 now
where the time goes in v3:
time: 77 us; the launch traced here: 76.8 us
  Pallas kernels  76.2 us (99%)
    pallas_call x1, Pallas kernels, body(): pl.pallas_call(kernel, out_shape=(jax.ShapeDtypeStruct((512, 512), BF16),...  74.2 us
    pallas_call x1, Pallas kernels, body(): pl.pallas_call(place_results, out_shape=tuple((jax.ShapeDtypeStruct(array...  2.01 us

profile of v3, /device:TPU:136, one launch (start us, length us, event | category | flops | bytes accessed | tf_op | source)
XLA Modules:
  0.0 76.8 jit_solution(3782975368193087725)
XLA Ops:
  0.6 74.2 %shard_map.84 = (bf16[512,512]{1,0:T(8,128)(2,1)}, bf16[64,512]{1,0:T(8,128)(2,1)}, bf16[64,512]{1,0:T(8,128)(2,1)}, bf16[128,512]{1,0:T(8,128)(2,1)}) custom-call(bf16[512,512]{1,0:T(8,128)(2,1)} %q_in.1, bf16[64,512]{1,0:T(8,128)(2,1)} %bitcast.4, bf16[64,512]{1,0:T(8,128)(2,1)} %bitcast.5, bf16[32,4096]{1,0:T(8,128)(2,1)} %g_in.1, bf16[128,512]{1,0:T(8,128)(2,1)} %w_in.1), custom_call_target="tpu_custom_call" | custom-call | flops 6000000000 | bytes 4000000 | tf_op jit(solution)/shard_map/pallas_call | solution.py:621
  74.8 2.0 %shard_map.85 = (bf16[512,512]{1,0:T(8,128)(2,1)}, bf16[64,512]{1,0:T(8,128)(2,1)}, bf16[64,512]{1,0:T(8,128)(2,1)}, bf16[128,512]{1,0:T(8,128)(2,1)}) custom-call(bf16[512,512]{1,0:T(8,128)(2,1)} %get-tuple-element.12.refs_0_, bf16[64,512]{1,0:T(8,128)(2,1)} %get-tuple-element.13.refs_1_, bf16[64,512]{1,0:T(8,128)(2,1)} %get-tuple-element.14.refs_2_, ...), custom_call_target="tpu_custom_call" | custom-call | bytes 1600000 | tf_op jit(solution)/shard_map/pallas_call | solution.py:675

commit v4 on v3

--- a/solution.py
+++ b/solution.py
@@ -611,12 +611,27 @@
 
 
 def place_results(*refs):
-    for i in range(4):
-        refs[i + 4][...] = refs[i][...]
+    arrays, results, held, sems = refs[0:4], refs[4:8], refs[8:12], refs[12]
+    pieces = [(0, slice(part * 256, part * 256 + 256)) for part in range(2)]
+    pieces += [(1, slice(0, 64)), (2, slice(0, 64)), (3, slice(0, 128))]
+    inward = [
+        pltpu.make_async_copy(arrays[i].at[rows], held[i].at[rows], sems.at[0, at])
+        for at, (i, rows) in enumerate(pieces)
+    ]
+    outward = [
+        pltpu.make_async_copy(held[i].at[rows], results[i].at[rows], sems.at[1, at])
+        for at, (i, rows) in enumerate(pieces)
+    ]
+    for copy in inward:
+        copy.start()
+    for arrival, copy in zip(inward, outward):
+        arrival.wait()
+        copy.start()
+    for copy in outward:
+        copy.wait()
 
 
 def body(queries, keys, values, grad_out, out_weight):
-    vmem = pl.BlockSpec(memory_space=pltpu.VMEM)
     anywhere = pl.BlockSpec(memory_space=pl.ANY)
     grad_q, grad_k, grad_v, grad_weight = pl.pallas_call(
         kernel,
@@ -675,8 +690,12 @@
     grad_q, grad_k, grad_v, grad_weight = pl.pallas_call(
         place_results,
         out_shape=tuple(jax.ShapeDtypeStruct(array.shape, array.dtype) for array in results),
-        in_specs=[vmem] * 4,
-        out_specs=(vmem,) * 4,
+        in_specs=[anywhere] * 4,
+        out_specs=(anywhere,) * 4,
+        scratch_shapes=[
+            *(pltpu.VMEM(array.shape, array.dtype) for array in results),
+            pltpu.SemaphoreType.DMA((2, 5)),
+        ],
         cost_estimate=pl.CostEstimate(flops=0, bytes_accessed=1_600_000, transcendentals=0),
     )(*results)
     return grad_q, grad_k.T, grad_v.T, grad_weight

time: 77 us -> 76.9 us (level)
  no operation moved by 1% of the time
where the time goes in v4:
time: 76.9 us; the launch traced here: 76.7 us
  Pallas kernels  76.1 us (99%)
    pallas_call x1, Pallas kernels, body(): pl.pallas_call(kernel, out_shape=(jax.ShapeDtypeStruct((512, 512), BF16),...  74.2 us
    pallas_call x1, Pallas kernels, body(): pl.pallas_call(place_results, out_shape=tuple((jax.ShapeDtypeStruct(array...  1.91 us

profile of v4, /device:TPU:136, one launch (start us, length us, event | category | flops | bytes accessed | tf_op | source)
XLA Modules:
  0.0 76.7 jit_solution(14166523835178328038)
XLA Ops:
  0.6 74.2 %shard_map.84 = (bf16[512,512]{1,0:T(8,128)(2,1)}, bf16[64,512]{1,0:T(8,128)(2,1)}, bf16[64,512]{1,0:T(8,128)(2,1)}, bf16[128,512]{1,0:T(8,128)(2,1)}) custom-call(bf16[512,512]{1,0:T(8,128)(2,1)} %q_in.1, bf16[64,512]{1,0:T(8,128)(2,1)} %bitcast.4, bf16[64,512]{1,0:T(8,128)(2,1)} %bitcast.5, bf16[32,4096]{1,0:T(8,128)(2,1)} %g_in.1, bf16[128,512]{1,0:T(8,128)(2,1)} %w_in.1), custom_call_target="tpu_custom_call" | custom-call | flops 6000000000 | bytes 4000000 | tf_op jit(solution)/shard_map/pallas_call | solution.py:636
  74.8 1.9 %shard_map.85 = (bf16[512,512]{1,0:T(8,128)(2,1)}, bf16[64,512]{1,0:T(8,128)(2,1)}, bf16[64,512]{1,0:T(8,128)(2,1)}, bf16[128,512]{1,0:T(8,128)(2,1)}) custom-call(bf16[512,512]{1,0:T(8,128)(2,1)} %get-tuple-element.12.refs_0_, bf16[64,512]{1,0:T(8,128)(2,1)} %get-tuple-element.13.refs_1_, bf16[64,512]{1,0:T(8,128)(2,1)} %get-tuple-element.14.refs_2_, ...), custom_call_target="tpu_custom_call" | custom-call | bytes 1600000 | tf_op jit(solution)/shard_map/pallas_call | solution.py:690
